TPU v7x, 128 devices: a whole 4x4x4 slice. The times are simulated.
128 devices in a mesh: chan: 8 (over y_hi, x), win: 4 (over z), freq: 4 (over y_lo, core).
Axes of the slice: x: 4, y: 4 (y_hi: 2, y_lo: 2; y = y_hi * 2 + y_lo), z: 4, core: 2. Of those that a mesh axis runs over, the one named last changes fastest.
Arguments:
- samples: bfloat16 [256, 512, 1024], P('win', 'chan', 'freq'), may hold values from -6 to 6
- partner: int32 [8, 8], replicated, may hold values from 0 to 7, as said below
Outputs:
- stacks: float32 [8, 8, 512, 64, 128], P('chan', None, 'freq', 'win')
Inputs may be any that keep to these rules, and one draw needn't show every extreme that they name: Each row partner[r] is an involution of the blocks 0 .. 7. The rounds form 1 pass of 8 consecutive rounds; within each pass every unordered pair of different blocks is matched in exactly one round, and in one round every block is matched with itself.
All inputs are finite; a program needn't handle non-finite values.
Results may differ from a plain program's by a relative error of at most 0.0038.
Values may be sent and summed in bfloat16 or wider, within the bound.
A program may use at most 256 MiB of HBM per device.

v0:
```python
import math

import jax
import jax.numpy as jnp
from jax import lax
from jax.sharding import PartitionSpec as P


def padded(block, sides, width):
    for axis, dim in sides:
        count = lax.axis_size(axis)
        forward = [(i, i + 1) for i in range(count - 1)]
        backward = [(target, source) for source, target in forward]
        low = lax.ppermute(
            lax.slice_in_dim(block, block.shape[dim] - width, None, axis=dim), axis, forward
        )
        high = lax.ppermute(lax.slice_in_dim(block, 0, width, axis=dim), axis, backward)
        block = jnp.concatenate([low, block, high], axis=dim)
    return block


def per_device(samples, partner):
    window_tally, block_rows, seg_local = samples.shape
    freq_count = lax.axis_size("freq")
    length = seg_local * freq_count
    bins_local = length // 2 // freq_count
    margin = length // 16
    first_bin = lax.axis_index("freq") * bins_local
    norm = 1.0 / math.sqrt(length)
    local_frequency_slots = first_bin + jnp.arange(bins_local, dtype=jnp.int32)
    phase = (
        jnp.arange(length, dtype=jnp.int32)[:, None] * local_frequency_slots[None, :] % length
    ).astype(jnp.float32)
    angle = phase * (2.0 * math.pi / length)
    table_cos = (jnp.cos(angle) * norm).astype(jnp.bfloat16)
    table_sin = (-jnp.sin(angle) * norm).astype(jnp.bfloat16)
    table_both = jnp.concatenate([table_cos, table_sin], axis=1)
    piece = lax.all_gather(samples, "freq", axis=2, tiled=True)
    rows_here = piece.shape[2]
    flat = piece.reshape(window_tally * block_rows, rows_here)
    spectrum = jnp.dot(flat, table_both, preferred_element_type=jnp.float32)
    fourier_inphase = spectrum[:, :bins_local]
    spec_im = spectrum[:, bins_local:]
    power = fourier_inphase * fourier_inphase + spec_im * spec_im
    extended_rows = padded(power, (("freq", 1),), margin)
    upper = jnp.arange(bins_local + 2 * margin, dtype=jnp.int32)[:, None]
    target = jnp.arange(bins_local, dtype=jnp.int32)[None, :]
    band = ((upper >= target) & (upper <= target + 2 * margin)).astype(jnp.float32)
    smooth = jnp.dot(
        extended_rows, band, precision=lax.Precision.HIGHEST, preferred_element_type=jnp.float32
    ) / (2 * margin + 1)
    scale = lax.rsqrt(smooth + 1e-06)
    white_re = (
        (fourier_inphase * scale).astype(jnp.bfloat16).reshape(window_tally, block_rows, bins_local)
    )
    white_im = (spec_im * scale).astype(jnp.bfloat16).reshape(window_tally, block_rows, bins_local)
    white = jnp.concatenate([white_re, white_im], axis=1).transpose(2, 0, 1)
    gathered = lax.all_gather(white[None], "chan", axis=0, tiled=True)
    own_block = lax.axis_index("chan")
    total_segments = window_tally * lax.axis_size("win")
    rounds = partner.shape[0]
    owned = []
    for step in range(rounds):
        other_block = lax.dynamic_index_in_dim(partner[step], own_block, 0, keepdims=False)
        other = lax.dynamic_index_in_dim(gathered, other_block, 0, keepdims=False)
        prod = jnp.einsum("fkc,fkd->fcd", white, other, preferred_element_type=jnp.float32)
        inphase_share = prod[:, :block_rows, :block_rows] + prod[:, block_rows:, block_rows:]
        imaginary_component = prod[:, :block_rows, block_rows:] - prod[:, block_rows:, :block_rows]
        owned.append(
            lax.psum_scatter(
                jnp.concatenate([inphase_share, imaginary_component], axis=2)
                * (1.0 / total_segments),
                "win",
                scatter_dimension=1,
                tiled=True,
            )
        )
    result = jnp.stack(owned, 0)
    return result[None]


def solution(mesh):
    in_specs = (P("win", "chan", "freq"), P())
    out_specs = P("chan", None, "freq", "win", None)
    return jax.shard_map(
        per_device, mesh=mesh, in_specs=in_specs, out_specs=out_specs, check_vma=False
    )
```

profile of v0, /device:TPU:0, one launch (start us, length us, event | category | flops | bytes accessed | tf_op | source)
XLA Modules:
  0.0 741.7 jit_solution(13440987230178828201)
XLA Ops:
  6.5 0.7 all-gather.4.cloned.1.call-update
  7.3 2.2 multiply_convert_fusion.3
  9.6 82.0 %all-gather.4.cloned.1.call-done = bf16[64,64,1024]{2,1,0:T(8,128)(2,1)} async-done(((bf16[64,64,256]{2,1,0:T(8,128)(2,1)}), bf16[64,64,1024]{2,1,0:T(8,128)(2,1)}) %all-gather.4.cloned.1.call-update) | async-done | bytes 8388624 | tf_op jit(solution)/shard_map/all_gather | solution.py:38
  91.6 5.8 convolution_bitcast_fusion
  97.3 0.2 multiply_add_fusion
  97.6 0.1 fusion.53
  97.7 3.5 collective-permute-start
  101.2 1.3 collective-permute-start.1
  102.5 0.9 collective-permute-done
  103.4 2.4 collective-permute-done.1
  105.8 3.2 multiply_convert_fusion.1
  109.0 1.6 copy.10
  110.6 3.0 copy.12
  113.6 1.6 copy.11
  115.2 3.7 copy.13
  118.9 4.2 maximum_bitcast_fusion
  123.1 0.2 reduce-scatter.9.cloned.1.call-start
  123.3 0.7 constant_dynamic-slice_fusion.6
  126.0 195.3 %all-gather.6.cloned.1.call-done = bf16[1024,64,128]{2,1,0:T(8,128)(2,1)} async-done(((bf16[128,64,128]{2,1,0:T(8,128)(2,1)}), bf16[1024,64,128]{2,1,0:T(8,128)(2,1)}) %all-gather.6.cloned.1.call-update) | async-done | bytes 16777232 | tf_op jit(solution)/shard_map/all_gather | solution.py:58
  321.3 7.0 fusion.21
  328.2 10.5 %slice_add_fusion.7 = (f32[128,64,64]{2,1,0:T(8,128)S(1)}, f32[128,64,64]{2,1,0:T(8,128)}) fusion(f32[128,128,128]{2,1,0:T(8,128)} %fusion.21), kind=kLoop, calls=%fused_computation.19 | loop fusion | flops 1048576 | bytes 12582912 | tf_op jit(solution)/shard_map/add | solution.py:67
  338.7 5.3 maximum_multiply_fusion
  344.0 0.0 reduce-scatter.11.cloned.1.call-start
  346.3 6.5 fusion.19
  352.8 10.4 %slice_add_fusion.6 = (f32[128,64,64]{2,1,0:T(8,128)S(1)}, f32[128,64,64]{2,1,0:T(8,128)}) fusion(f32[128,128,128]{2,1,0:T(8,128)} %fusion.19), kind=kLoop, calls=%fused_computation.17 | loop fusion | flops 1048576 | bytes 12582912 | tf_op jit(solution)/shard_map/add | solution.py:67
  363.2 5.5 maximum_multiply_fusion.1
  368.7 0.3 reduce-scatter.13.cloned.1.call-start
  368.9 0.6 constant_dynamic-slice_fusion.4
  371.5 6.4 fusion.17
  377.8 10.5 %slice_add_fusion.5 = (f32[128,64,64]{2,1,0:T(8,128)S(1)}, f32[128,64,64]{2,1,0:T(8,128)}) fusion(f32[128,128,128]{2,1,0:T(8,128)} %fusion.17), kind=kLoop, calls=%fused_computation.15 | loop fusion | flops 1048576 | bytes 12582912 | tf_op jit(solution)/shard_map/add | solution.py:67
  388.4 5.4 maximum_multiply_fusion.2
  395.5 6.5 fusion.15
  402.0 10.5 %slice_add_fusion.4 = (f32[128,64,64]{2,1,0:T(8,128)S(1)}, f32[128,64,64]{2,1,0:T(8,128)}) fusion(f32[128,128,128]{2,1,0:T(8,128)} %fusion.15), kind=kLoop, calls=%fused_computation.13 | loop fusion | flops 1048576 | bytes 12582912 | tf_op jit(solution)/shard_map/add | solution.py:67
  412.5 5.4 maximum_multiply_fusion.3
  417.9 0.4 reduce-scatter.17.cloned.1.call-start
  418.4 0.7 constant_dynamic-slice_fusion.2
  421.0 6.4 fusion.13
  427.4 10.6 %slice_add_fusion.3 = (f32[128,64,64]{2,1,0:T(8,128)S(1)}, f32[128,64,64]{2,1,0:T(8,128)}) fusion(f32[128,128,128]{2,1,0:T(8,128)} %fusion.13), kind=kLoop, calls=%fused_computation.11 | loop fusion | flops 1048576 | bytes 12582912 | tf_op jit(solution)/shard_map/add | solution.py:67
  438.0 5.4 maximum_multiply_fusion.4
  443.4 0.0 reduce-scatter.19.cloned.1.call-start
  445.5 6.3 fusion.11
  451.8 10.5 %slice_add_fusion.2 = (f32[128,64,64]{2,1,0:T(8,128)S(1)}, f32[128,64,64]{2,1,0:T(8,128)}) fusion(f32[128,128,128]{2,1,0:T(8,128)} %fusion.11), kind=kLoop, calls=%fused_computation.9 | loop fusion | flops 1048576 | bytes 12582912 | tf_op jit(solution)/shard_map/add | solution.py:67
  462.3 5.3 maximum_multiply_fusion.5
  467.6 0.2 reduce-scatter.21.cloned.1.call-start
  467.9 0.7 constant_dynamic-slice_fusion
  470.5 6.3 fusion.9
  476.8 10.6 %slice_add_fusion.1 = (f32[128,64,64]{2,1,0:T(8,128)S(1)}, f32[128,64,64]{2,1,0:T(8,128)}) fusion(f32[128,128,128]{2,1,0:T(8,128)} %fusion.9), kind=kLoop, calls=%fused_computation.7 | loop fusion | flops 1048576 | bytes 12582912 | tf_op jit(solution)/shard_map/add | solution.py:67
  487.4 5.3 maximum_multiply_fusion.6
  494.6 6.3 fusion.7
  500.9 10.6 %slice_add_fusion = (f32[128,64,64]{2,1,0:T(8,128)S(1)}, f32[128,64,64]{2,1,0:T(8,128)}) fusion(f32[128,128,128]{2,1,0:T(8,128)} %fusion.7), kind=kLoop, calls=%fused_computation.5 | loop fusion | flops 1048576 | bytes 12582912 | tf_op jit(solution)/shard_map/add | solution.py:67
  511.4 5.3 maximum_multiply_fusion.7
  516.8 2.3 bitcast_dynamic-update-slice_fusion.7
  519.0 2.3 bitcast_dynamic-update-slice_fusion.6
  521.3 2.3 bitcast_dynamic-update-slice_fusion.5
  523.6 12.5 %reduce-scatter.15.cloned.1.call-done = f32[128,16,128]{2,1,0:T(8,128)} async-done(((f32[128,64,128]{2,1,0:T(8,128)}), f32[128,16,128]{2,1,0:T(8,128)}) %reduce-scatter.15.cloned.1.call-update) | async-done | bytes 1048592 | tf_op jit(solution)/shard_map/reduce_scatter | solution.py:70
  536.1 2.3 bitcast_dynamic-update-slice_fusion.4
  538.3 46.8 %reduce-scatter.17.cloned.1.call-done = f32[128,16,128]{2,1,0:T(8,128)} async-done(((f32[128,64,128]{2,1,0:T(8,128)}), f32[128,16,128]{2,1,0:T(8,128)}) %reduce-scatter.17.cloned.1.call-update) | async-done | bytes 1048592 | tf_op jit(solution)/shard_map/reduce_scatter | solution.py:70
  585.1 2.3 bitcast_dynamic-update-slice_fusion.3
  587.4 46.9 %reduce-scatter.19.cloned.1.call-done = f32[128,16,128]{2,1,0:T(8,128)} async-done(((f32[128,64,128]{2,1,0:T(8,128)}), f32[128,16,128]{2,1,0:T(8,128)}) %reduce-scatter.19.cloned.1.call-update) | async-done | bytes 1048592 | tf_op jit(solution)/shard_map/reduce_scatter | solution.py:70
  634.3 2.3 bitcast_dynamic-update-slice_fusion.2
  636.6 46.8 %reduce-scatter.21.cloned.1.call-done = f32[128,16,128]{2,1,0:T(8,128)} async-done(((f32[128,64,128]{2,1,0:T(8,128)}), f32[128,16,128]{2,1,0:T(8,128)}) %reduce-scatter.21.cloned.1.call-update) | async-done | bytes 1048592 | tf_op jit(solution)/shard_map/reduce_scatter | solution.py:70
  683.3 2.3 bitcast_dynamic-update-slice_fusion.1
  685.6 46.8 %reduce-scatter.23.cloned.1.call-done = f32[128,16,128]{2,1,0:T(8,128)} async-done(((f32[128,64,128]{2,1,0:T(8,128)}), f32[128,16,128]{2,1,0:T(8,128)}) %reduce-scatter.23.cloned.1.call-update) | async-done | bytes 1048592 | tf_op jit(solution)/shard_map/reduce_scatter | solution.py:70
  732.4 2.3 bitcast_dynamic-update-slice_fusion
  (23 shorter events, 0.3 us)
Async XLA Ops:
  6.5 85.0 %all-gather.4.cloned.1.call-start = ((), (), s32[]{:S(2)}) async-start(), calls=%async_computation.8 | async-start | bytes 10485760 | tf_op jit(solution)/shard_map/all_gather | solution.py:38
  7.3 314.0 %all-gather.6.cloned.1.call-start = ((), (), s32[]{:S(2)}) async-start(), calls=%async_computation.17 | async-start | bytes 18874368 | tf_op jit(solution)/shard_map/all_gather | solution.py:58
  97.7 5.7 collective-permute-start
  101.2 4.6 collective-permute-start.1
  118.9 4.4 copy-start.1
  123.1 393.7 %reduce-scatter.9.cloned.1.call-start = ((), (), s32[]{:S(2)}) async-start(), calls=%async_computation.9 | async-start | bytes 5242880 | tf_op jit(solution)/shard_map/reduce_scatter | solution.py:70
  344.0 2.3 copy-start
  344.0 175.0 %reduce-scatter.11.cloned.1.call-start = ((), (), s32[]{:S(2)}) async-start(), calls=%async_computation.10 | async-start | bytes 5242880 | tf_op jit(solution)/shard_map/reduce_scatter | solution.py:70
  368.7 152.7 %reduce-scatter.13.cloned.1.call-start = ((), (), s32[]{:S(2)}) async-start(), calls=%async_computation.11 | async-start | bytes 5242880 | tf_op jit(solution)/shard_map/reduce_scatter | solution.py:70
  393.8 142.3 %reduce-scatter.15.cloned.1.call-start = ((), (), s32[]{:S(2)}) async-start(), calls=%async_computation.12 | async-start | bytes 5242880 | tf_op jit(solution)/shard_map/reduce_scatter | solution.py:70
  417.9 167.2 %reduce-scatter.17.cloned.1.call-start = ((), (), s32[]{:S(2)}) async-start(), calls=%async_computation.13 | async-start | bytes 5242880 | tf_op jit(solution)/shard_map/reduce_scatter | solution.py:70
  443.4 190.9 %reduce-scatter.19.cloned.1.call-start = ((), (), s32[]{:S(2)}) async-start(), calls=%async_computation.14 | async-start | bytes 5242880 | tf_op jit(solution)/shard_map/reduce_scatter | solution.py:70
  467.6 215.7 %reduce-scatter.21.cloned.1.call-start = ((), (), s32[]{:S(2)}) async-start(), calls=%async_computation.15 | async-start | bytes 5242880 | tf_op jit(solution)/shard_map/reduce_scatter | solution.py:70
  492.7 239.7 %reduce-scatter.23.cloned.1.call-start = ((), (), s32[]{:S(2)}) async-start(), calls=%async_computation.16 | async-start | bytes 5242880 | tf_op jit(solution)/shard_map/reduce_scatter | solution.py:70
Sparse Core Ops, SparseCore 0:
  9.0 82.5 all-gather.3
  123.2 198.0 all-gather.5
  344.1 44.9 reduce-scatter.8
  391.5 46.5 reduce-scatter.10
  440.4 46.5 reduce-scatter.12
  489.4 46.5 reduce-scatter.14
  538.5 46.5 reduce-scatter.16
  587.7 46.5 reduce-scatter.18
  636.7 46.5 reduce-scatter.20
  685.7 46.5 reduce-scatter.22
where the time goes:
time: 751 us; the launch traced here: 742 us
  waiting for transfers between devices  481 us (64%)
  other arithmetic  134 us (18%)
  matrix products  60.6 us (8%)
  local copies, waits for them, and re-layouts  30.8 us (4%)
  between operations  29.4 us (4%)
    reduce_scatter x8, waiting for transfers between devices, per_device(): lax.psum_scatter(jnp.concatenate([inphase_share, imaginary_component], ax...  200 us
    all_gather x1, waiting for transfers between devices, per_device(): gathered = lax.all_gather(white[None], 'chan', axis=0, tiled=True)  195 us
    add x8, other arithmetic, per_device(): prod[:, :block_rows, :block_rows] + prod[:, block_rows:, block_rows:]  84.1 us
    all_gather x1, waiting for transfers between devices, per_device(): piece = lax.all_gather(samples, 'freq', axis=2, tiled=True)  82 us
    dot_general x8, matrix products, per_device(): jnp.einsum('fkc,fkd->fcd', white, other, preferred_element_type=jnp.float32)  51.7 us
    mul x8, other arithmetic, per_device(): jnp.concatenate([inphase_share, imaginary_component], axis=2)  42.8 us
    unnamed x11, local copies, waits for them, and re-layouts  15.9 us
  transfers between devices with their start and end apart: 12, of which 9 were waited for; matrix products, arithmetic and copies ran while one was open for 24% of the time, Pallas kernels for 0%

commit v1 on v0

v1 whole, which is shorter than its diff:
```python
import functools
import math

import jax
import jax.numpy as jnp
import ml_dtypes
import numpy as np
from jax import lax
from jax.experimental import pallas as pl
from jax.experimental.pallas import tpu as pltpu
from jax.sharding import PartitionSpec as P

MESH = pl.DeviceIdType.MESH
NT = (((1,), (1,)), ((), ()))

LENGTH = 1024
BINS = 512
MARGIN = 64
SEGS = 64
SEGMENTS = 256
BLOCK = 64
CHANS = 512
ROWS = 1024


def tables():
    n = np.arange(LENGTH)[None, :]
    f = np.arange(BINS)[:, None]
    angle = (n * f % LENGTH) * (2.0 * math.pi / LENGTH)
    both = np.concatenate([np.cos(angle), -np.sin(angle)], axis=0) / math.sqrt(LENGTH)
    return both.astype(np.float32).astype(ml_dtypes.bfloat16)


def position():
    chan, win, freq = (lax.axis_index(name) for name in ("chan", "win", "freq"))
    return chan // 4, chan % 4, win, freq // 2, freq % 2


def peer_all(i, s):
    y_hi, x, z, y_lo, core = position()
    y = (y_hi * 2 + y_lo + i // 2 % 2 + 2 * s) % 4
    return (
        (y // 2) * 4 + (x + i // 4 % 4 + 2 * s) % 4,
        (z + i // 16 + 2 * s) % 4,
        y % 2 * 2 + (core + i % 2) % 2,
    )


def peer_rows(i, s):
    y_hi, x, z, y_lo, core = position()
    return (
        (y_hi + s) % 2 * 4 + (x + i % 4 + 2 * s) % 4,
        (z + i // 4 + 2 * s) % 4,
        y_lo * 2 + core,
    )


def each_peer(half, peer, act):
    act(peer(0, 1))

    def body(i, carry):
        act(peer(i, 0))
        act(peer(i, 1))
        return carry

    lax.fori_loop(1, half, body, 0)


def main_kernel(
    x_ref, table_ref, out_ref,
    table, got, wide, rows, spec, high, low, mixed, white, a_mat, b_mat, sums,
    table_sem, send1, recv1, send3, recv3, send5, recv5,
):
    chan, win, freq = (lax.axis_index(name) for name in ("chan", "win", "freq"))
    holder = chan * 4 + win
    piece = x_ref.shape[2]
    take_table = pltpu.make_async_copy(table_ref, table, table_sem)
    take_table.start()

    barrier = pltpu.get_barrier_semaphore()
    each_peer(64, peer_all, lambda d: pl.semaphore_signal(
        barrier, inc=1, device_id=d, device_id_type=MESH))
    pl.semaphore_wait(barrier, 127)

    here = pl.ds(pl.multiple_of(freq * piece, piece), piece)
    for step in (2, 3, 1):
        k = (freq + step) % 4
        pltpu.make_async_remote_copy(
            src_ref=x_ref.at[:, pl.ds(pl.multiple_of(k * 16, 16), 16), :],
            dst_ref=got.at[:, :, here],
            send_sem=send1, recv_sem=recv1,
            device_id=(chan, win, k), device_id_type=MESH,
        ).start()
    pltpu.make_async_copy(
        x_ref.at[:, pl.ds(pl.multiple_of(freq * 16, 16), 16), :], got.at[:, :, here], recv1
    ).start()
    pltpu.make_async_copy(got, got, recv1).wait()

    def reorder(c, carry):
        at = pl.ds(pl.multiple_of(c * 128, 128), 128)
        wide[...] = got[:, :, at].astype(jnp.float32).reshape(ROWS, 128)
        for ch in range(16):
            rows[ch * 64:(ch + 1) * 64, at] = wide[pl.ds(ch, 64, stride=16), :].astype(jnp.bfloat16)
        return carry

    lax.fori_loop(0, LENGTH // 128, reorder, 0)
    take_table.wait()

    def transform(t, carry):
        at = pl.ds(pl.multiple_of(t * 128, 128), 128)
        spec[at, :] = lax.dot_general(
            table[at, :], rows[...], NT, preferred_element_type=jnp.float32)
        return carry

    lax.fori_loop(0, 2 * BINS // 128, transform, 0)

    def powers(t, carry):
        at = pl.ds(pl.multiple_of(t * 32, 32), 32)
        im_at = pl.ds(pl.multiple_of(BINS + t * 32, 32), 32)
        re, im = spec[at, :], spec[im_at, :]
        power = re * re + im * im
        top = power.astype(jnp.bfloat16)
        high[at, :] = top
        low[at, :] = (power - top.astype(jnp.float32)).astype(jnp.bfloat16)
        return carry

    lax.fori_loop(0, BINS // 32, powers, 0)

    left = lax.broadcasted_iota(jnp.int32, (128, 128), 1) < 64

    def whiten(t, carry):
        first = t * 128
        start = jnp.clip(first - 64, 0, BINS - 256)
        window = pl.ds(pl.multiple_of(start, 64), 256)
        apart = (lax.broadcasted_iota(jnp.int32, (128, 256), 1) + start) - (
            lax.broadcasted_iota(jnp.int32, (128, 256), 0) + first)
        band = jnp.where((apart >= -MARGIN) & (apart <= MARGIN), 1.0, 0.0).astype(jnp.bfloat16)
        smooth = (
            jnp.dot(band, high[window, :], preferred_element_type=jnp.float32)
            + jnp.dot(band, low[window, :], preferred_element_type=jnp.float32)
        ) / (2 * MARGIN + 1)
        scale = lax.rsqrt(smooth + 1e-06)
        re = spec[pl.ds(pl.multiple_of(first, 128), 128), :] * scale
        im = spec[pl.ds(pl.multiple_of(BINS + first, 128), 128), :] * scale
        for c in range(8):
            a, b = re[:, c * 128:(c + 1) * 128], im[:, c * 128:(c + 1) * 128]
            mixed[pl.ds(2 * c, 128, stride=16), :] = jnp.where(left, a, pltpu.roll(b, 64, 1))
            mixed[pl.ds(2 * c + 1, 128, stride=16), :] = jnp.where(left, pltpu.roll(a, 64, 1), b)
        white[pl.ds(pl.multiple_of(first, 128), 128)] = (
            mixed[...].reshape(128, 16, 128).astype(jnp.bfloat16))
        return carry

    lax.fori_loop(0, BINS // 128, whiten, 0)

    place_ch = pl.ds(pl.multiple_of(chan * 64 + freq * 16, 16), 16)
    place_k = pl.ds(pl.multiple_of(win * 128, 128), 128)

    def send_white(d):
        pltpu.make_async_remote_copy(
            src_ref=white.at[pl.ds(d[2] * 128 + (d[0] * 4 + d[1]) * 4, 4)],
            dst_ref=a_mat.at[:, place_ch, place_k],
            send_sem=send3, recv_sem=recv3, device_id=d, device_id_type=MESH,
        ).start()

    each_peer(64, peer_all, send_white)
    pltpu.make_async_copy(
        white.at[pl.ds(freq * 128 + holder * 4, 4)], a_mat.at[:, place_ch, place_k], recv3
    ).start()
    pltpu.make_async_copy(a_mat, a_mat, recv3).wait()

    sign = jnp.where(lax.broadcasted_iota(jnp.int32, (64, 128), 1) < 64, 1.0, -1.0)

    def cross(b, carry):
        def turn(q, c):
            block = a_mat[b, pl.ds(pl.multiple_of(q * 64, 64), 64), :]
            b_mat[pl.ds(pl.multiple_of(q * 128, 128), 64), :] = block
            for w in range(4):
                part = block[:, w * 128:(w + 1) * 128].astype(jnp.float32)
                b_mat[pl.ds(pl.multiple_of(q * 128 + 64, 64), 64), w * 128:(w + 1) * 128] = (
                    pltpu.roll(part, 64, 1) * sign).astype(jnp.bfloat16)
            return c

        lax.fori_loop(0, 8, turn, 0)

        def multiply(m, c):
            tile = lax.dot_general(
                a_mat[b, pl.ds(pl.multiple_of(m * 128, 128), 128), :], b_mat[...], NT,
                preferred_element_type=jnp.float32)
            tile = (tile * (1.0 / SEGMENTS)).astype(jnp.bfloat16)
            for q in range(8):
                sums[pl.ds(m * 8, 8), b, q] = tile[:, q * 128:(q + 1) * 128].reshape(8, 16, 128)
            return c

        lax.fori_loop(0, 4, multiply, 0)

        def send_sums(d):
            pltpu.make_async_remote_copy(
                src_ref=sums.at[d[0] * 4 + d[1], b],
                dst_ref=out_ref.at[holder * 4 + b],
                send_sem=send5, recv_sem=recv5, device_id=d, device_id_type=MESH,
            ).start()

        each_peer(16, peer_rows, send_sums)
        pltpu.make_async_copy(sums.at[holder, b], out_ref.at[holder * 4 + b], recv5).start()
        return carry

    lax.fori_loop(0, 4, cross, 0)

    pltpu.make_async_copy(out_ref, out_ref, recv5).wait()
    three = pl.ds(0, 48)
    pltpu.make_async_copy(got.at[pl.ds(0, 48)], got.at[pl.ds(0, 48)], send1).wait()
    pltpu.make_async_copy(white.at[pl.ds(0, 508)], white.at[pl.ds(0, 508)], send3).wait()
    pltpu.make_async_copy(sums.at[pl.ds(0, 31)], sums.at[pl.ds(0, 31)], send5).wait()


def order_kernel(partner_ref, in_ref, out_ref):
    chan = lax.axis_index("chan")
    for r in range(8):
        out_ref[0, r] = in_ref[:, partner_ref[r, chan]].astype(jnp.float32)


def per_device(samples, partner):
    table = jnp.asarray(tables())
    sums = pl.pallas_call(
        main_kernel,
        out_shape=jax.ShapeDtypeStruct((128, 8, 16, 128), jnp.bfloat16),
        in_specs=[pl.BlockSpec(memory_space=pl.ANY)] * 2,
        out_specs=pl.BlockSpec(memory_space=pl.ANY),
        scratch_shapes=[
            pltpu.VMEM((2 * BINS, LENGTH), jnp.bfloat16),
            pltpu.VMEM((SEGS, 16, LENGTH), jnp.bfloat16),
            pltpu.VMEM((ROWS, 128), jnp.float32),
            pltpu.VMEM((ROWS, LENGTH), jnp.bfloat16),
            pltpu.VMEM((2 * BINS, ROWS), jnp.float32),
            pltpu.VMEM((BINS, ROWS), jnp.bfloat16),
            pltpu.VMEM((BINS, ROWS), jnp.bfloat16),
            pltpu.VMEM((128 * 16, 128), jnp.float32),
            pltpu.VMEM((BINS, 16, 128), jnp.bfloat16),
            pltpu.VMEM((4, CHANS, 512), jnp.bfloat16),
            pltpu.VMEM((2 * CHANS, 512), jnp.bfloat16),
            pltpu.VMEM((32, 4, 8, 16, 128), jnp.bfloat16),
        ] + [pltpu.SemaphoreType.DMA] * 7,
        compiler_params=pltpu.CompilerParams(
            collective_id=0, has_side_effects=True, vmem_limit_bytes=48 * 2**20),
        name="spectra",
    )(samples, table)
    chunk = 16
    return pl.pallas_call(
        order_kernel,
        out_shape=jax.ShapeDtypeStruct((1, 8, 128, 16, 128), jnp.float32),
        grid_spec=pltpu.PrefetchScalarGridSpec(
            num_scalar_prefetch=1,
            grid=(128 // chunk,),
            in_specs=[pl.BlockSpec((chunk, 8, 16, 128), lambda i, part: (i, 0, 0, 0))],
            out_specs=pl.BlockSpec((1, 8, chunk, 16, 128), lambda i, part: (0, 0, i, 0, 0)),
        ),
        compiler_params=pltpu.CompilerParams(vmem_limit_bytes=16 * 2**20),
        name="order",
    )(partner, sums)


def solution(mesh):
    in_specs = (P("win", "chan", "freq"), P())
    out_specs = P("chan", None, "freq", "win", None)
    return jax.shard_map(
        per_device, mesh=mesh, in_specs=in_specs, out_specs=out_specs, check_vma=False
    )
```

time: 751 us -> 140 us (0.19); the launches traced: 742 us -> 139 us
  waiting for transfers between devices: 481 us -> 0 us
  other arithmetic: 134 us -> 0 us
  Pallas kernels: 0 us -> 133 us
  matrix products: 60.6 us -> 0 us
  between operations: 29.4 us -> 0.03 us
  local copies, waits for them, and re-layouts: 30.8 us -> 5.37 us
    all_gather x2 -> x0, waiting for transfers between devices: 277 us -> none  [the longest x1 195 us: per_device(): gathered = lax.all_gather(white[None], 'chan', axis=0, tiled=True)]
    reduce_scatter x8 -> x0, waiting for transfers between devices: 200 us -> none  [per_device(): lax.psum_scatter(jnp.concatenate([inphase_share, imaginary_component], ax...]
    pallas_call x0 -> x2, Pallas kernels: none -> 133 us  [the longest x1 128 us: per_device(): pl.pallas_call(main_kernel, out_shape=jax.ShapeDtypeStruct((128, 8, 16, 1...]
    add x11 -> x0, other arithmetic: 84.4 us -> none  [the longest x8 84.1 us: per_device(): prod[:, :block_rows, :block_rows] + prod[:, block_rows:, block_rows:]]
    dot_general x10 -> x0, matrix products: 60.6 us -> none  [the longest x8 51.7 us: per_device(): jnp.einsum('fkc,fkd->fcd', white, other, preferred_element_type=jnp.float32)]
    mul x8 -> x0, other arithmetic: 42.8 us -> none  [per_device(): jnp.concatenate([inphase_share, imaginary_component], axis=2)]
    unnamed x11 -> x8, local copies, waits for them, and re-layouts: 15.9 us -> 5.37 us
  transfers between devices with their start and end apart: 12 -> 0, of which waited for: 9 -> 0; matrix products, arithmetic and copies ran while one was open for 24% -> 0% of each run, Pallas kernels for 0% -> 0%
where the time goes in v1:
time: 140 us; the launch traced here: 139 us
  Pallas kernels  133 us (95%)
  local copies, waits for them, and re-layouts  5.37 us (4%)
    pallas_call x1, Pallas kernels, per_device(): pl.pallas_call(main_kernel, out_shape=jax.ShapeDtypeStruct((128, 8, 16, 1...  128 us
    unnamed x8, local copies, waits for them, and re-layouts  5.37 us
    pallas_call x1, Pallas kernels, per_device(): pl.pallas_call(order_kernel, out_shape=jax.ShapeDtypeStruct((1, 8, 128, 1...  5.15 us

profile of v1, /device:TPU:0, one launch (start us, length us, event | category | flops | bytes accessed | tf_op | source)
XLA Modules:
  0.0 138.7 jit_solution(631949936816751574)
XLA Ops:
  0.0 0.0 copy-start.1
  0.0 1.6 %copy-done.1 = bf16[64,64,256]{2,1,0:T(8,128)(2,1)S(1)} copy-done((bf16[64,64,256]{2,1,0:T(8,128)(2,1)S(1)}, bf16[64,64,256]{2,1,0:T(8,128)(2,1)}, u32[]{:S(2)}) %copy-start.1) | copy-done | bytes 2097176
  1.6 0.0 copy-start.2
  1.6 1.6 %copy-done.2 = bf16[1024,1024]{1,0:T(8,128)(2,1)S(1)} copy-done((bf16[1024,1024]{1,0:T(8,128)(2,1)S(1)}, bf16[1024,1024]{1,0:T(8,128)(2,1)}, u32[]{:S(2)}) %copy-start.2) | copy-done | bytes 2097176
  3.2 0.0 copy-start.3
  3.2 128.1 %spectra.1.in_ref = bf16[128,8,16,128]{3,2,1,0:T(8,128)(2,1)} custom-call(bf16[64,64,256]{2,1,0:T(8,128)(2,1)S(1)} %copy-done.1, bf16[1024,1024]{1,0:T(8,128)(2,1)S(1)} %copy-done.2), custom_call_target="tpu_custom_call" | custom-call | tf_op jit(solution)/shard_map/spectra/pallas_call | solution.py:224
  131.3 0.0 copy-done.3
  131.3 0.0 copy-start
  131.3 2.2 %copy-done = bf16[128,8,16,128]{3,2,1,0:T(8,128)(2,1)S(1)} copy-done((bf16[128,8,16,128]{3,2,1,0:T(8,128)(2,1)S(1)}, bf16[128,8,16,128]{3,2,1,0:T(8,128)(2,1)}, u32[]{:S(2)}) %copy-start) | copy-done | bytes 4194328
  133.5 5.1 %order.1 = f32[1,8,128,16,128]{4,3,2,1,0:T(8,128)} custom-call(s32[8,8]{1,0:T(8,128)S(1)} %copy-done.3, bf16[128,8,16,128]{3,2,1,0:T(8,128)(2,1)S(1)} %copy-done), custom_call_target="tpu_custom_call" | custom-call | tf_op jit(solution)/shard_map/order/pallas_call | solution.py:248
Async XLA Ops:
  0.0 1.6 %copy-start.1 = (bf16[64,64,256]{2,1,0:T(8,128)(2,1)S(1)}, bf16[64,64,256]{2,1,0:T(8,128)(2,1)}, u32[]{:S(2)}) copy-start(bf16[64,64,256]{2,1,0:T(8,128)(2,1)} %x_ref.1) | copy-start | bytes 6291460
  1.6 1.6 %copy-start.2 = (bf16[1024,1024]{1,0:T(8,128)(2,1)S(1)}, bf16[1024,1024]{1,0:T(8,128)(2,1)}, u32[]{:S(2)}) copy-start(bf16[1024,1024]{1,0:T(8,128)(2,1)} %constant.2.clone.table_ref) | copy-start | bytes 6291460
  3.2 128.1 %copy-start.3 = (s32[8,8]{1,0:T(8,128)S(1)}, s32[8,8]{1,0:T(8,128)}, u32[]{:S(2)}) copy-start(s32[8,8]{1,0:T(8,128)} %partner_ref.1) | copy-start | bytes 772
  131.3 2.2 %copy-start = (bf16[128,8,16,128]{3,2,1,0:T(8,128)(2,1)S(1)}, bf16[128,8,16,128]{3,2,1,0:T(8,128)(2,1)}, u32[]{:S(2)}) copy-start(bf16[128,8,16,128]{3,2,1,0:T(8,128)(2,1)} %spectra.1.in_ref) | copy-start | bytes 12582916

commit v2 on v1

v2 whole, which is shorter than its diff:
```python
import functools
import math

import jax
import jax.numpy as jnp
import ml_dtypes
import numpy as np
from jax import lax
from jax.experimental import pallas as pl
from jax.experimental.pallas import tpu as pltpu
from jax.sharding import PartitionSpec as P

MESH = pl.DeviceIdType.MESH
NT = (((1,), (1,)), ((), ()))

LENGTH = 1024
BINS = 512
MARGIN = 64
SEGS = 64
SEGMENTS = 256
BLOCK = 64
CHANS = 512
ROWS = 1024


def tables():
    n = np.arange(LENGTH)[None, :]
    f = np.arange(BINS)[:, None]
    angle = (n * f % LENGTH) * (2.0 * math.pi / LENGTH)
    both = np.concatenate([np.cos(angle), -np.sin(angle)], axis=0) / math.sqrt(LENGTH)
    return both.astype(np.float32).astype(ml_dtypes.bfloat16)


def position():
    chan, win, freq = (lax.axis_index(name) for name in ("chan", "win", "freq"))
    return chan // 4, chan % 4, win, freq // 2, freq % 2


def peer_all(i, s):
    y_hi, x, z, y_lo, core = position()
    y = (y_hi * 2 + y_lo + i // 2 % 2 + 2 * s) % 4
    return (
        (y // 2) * 4 + (x + i // 4 % 4 + 2 * s) % 4,
        (z + i // 16 + 2 * s) % 4,
        y % 2 * 2 + (core + i % 2) % 2,
    )


def peer_rows(i, s):
    y_hi, x, z, y_lo, core = position()
    return (
        (y_hi + s) % 2 * 4 + (x + i % 4 + 2 * s) % 4,
        (z + i // 4 + 2 * s) % 4,
        y_lo * 2 + core,
    )


def peer_share(k, i, s):
    y_hi, x, z, y_lo, core = position()
    y = (y_hi * 2 + (y_lo * 2 + core + k) % 4 // 2 + 2 * s) % 4
    return (
        y // 2 * 4 + (x + i % 4 + 2 * s) % 4,
        (z + i // 4 + 2 * s) % 4,
        (y_lo * 2 + core + k) % 4,
    )


def each_peer(half, peer, act, skip_own=True):
    if skip_own is not True:

        @pl.when(jnp.logical_not(skip_own))
        def _():
            act(peer(0, 0))

    act(peer(0, 1))

    def body(i, carry):
        act(peer(i, 0))
        act(peer(i, 1))
        return carry

    lax.fori_loop(1, half, body, 0)


def main_kernel(
    x_ref, table_ref, out_ref,
    table, got, wide, rows, spec, high, low, mixed, white, a_mat, b_mat, sums,
    table_sem, send1, recv1, send3, recv3, send5, recv5, in_sem,
):
    chan, win, freq = (lax.axis_index(name) for name in ("chan", "win", "freq"))
    holder = chan * 4 + win
    piece = x_ref.shape[2]
    take_table = pltpu.make_async_copy(table_ref, table, table_sem)
    take_table.start()

    barrier = pltpu.get_barrier_semaphore()
    y_hi, x, z, y_lo, core = position()
    along_x = [(y_hi * 4 + (x + i) % 4, win, freq) for i in (1, 2, 3)]
    along_z = [(chan, (z + i) % 4, freq) for i in (1, 2, 3)]
    along_freq = [(chan, win, (freq + i) % 4) for i in (1, 2, 3)]

    def tell(semaphore, devices):
        for d in devices:
            pl.semaphore_signal(semaphore, inc=1, device_id=d, device_id_type=MESH)

    tell(barrier, along_freq + along_x + along_z + [((1 - y_hi) * 4 + x, win, freq)])
    pl.semaphore_wait(barrier, 10)

    def across(i):
        return (y_lo + i // 2) % 2 * 2 + (core + i % 2) % 2

    def stretch(k, size=1):
        return pl.ds(pl.multiple_of(k * piece, size * piece), size * piece)

    pltpu.make_async_copy(
        x_ref.at[:, pl.ds(pl.multiple_of(freq * 16, 16), 16), :],
        got.at[:, :, stretch(freq)], recv1.at[0],
    ).start()
    for i in (2, 1, 3):
        k = across(i)
        pltpu.make_async_remote_copy(
            src_ref=x_ref.at[:, pl.ds(pl.multiple_of(k * 16, 16), 16), :],
            dst_ref=got.at[:, :, stretch(freq)],
            send_sem=send1, recv_sem=recv1.at[i],
            device_id=(chan, win, k), device_id_type=MESH,
        ).start()

    def arrived(i):
        part = got.at[:, :, stretch(across(i))]
        pltpu.make_async_copy(part, part, recv1.at[i]).wait()

    def reorder(k):
        def body(c, carry):
            at = pl.ds(pl.multiple_of(k * piece + c * 128, 128), 128)
            wide[...] = got[:, :, at].astype(jnp.float32).reshape(ROWS, 128)
            for ch in range(16):
                rows[ch * 64:(ch + 1) * 64, at] = (
                    wide[pl.ds(ch, 64, stride=16), :].astype(jnp.bfloat16))
            return carry

        lax.fori_loop(0, piece // 128, body, 0)

    def transform(k, size, first):
        span = stretch(k, size)

        def body(t, carry):
            at = pl.ds(pl.multiple_of(t * 256, 256), 256)
            term = lax.dot_general(
                table[:, span], rows[at, span], NT, preferred_element_type=jnp.float32)
            spec[:, at] = term if first else spec[:, at] + term
            return carry

        lax.fori_loop(0, ROWS // 256, body, 0)

    tell(in_sem.at[0], along_z)
    take_table.wait()
    for i in (0, 1):
        arrived(i)
        reorder(across(i))
    pl.semaphore_wait(in_sem.at[0], 3)
    tell(in_sem.at[1], along_x)
    transform(y_lo * 2, 2, True)
    pl.semaphore_wait(in_sem.at[1], 3)
    tell(in_sem.at[2], along_freq)
    for i in (2, 3):
        arrived(i)
        reorder(across(i))
        transform(across(i), 1, False)

    def powers(t, carry):
        at = pl.ds(pl.multiple_of(t * 32, 32), 32)
        im_at = pl.ds(pl.multiple_of(BINS + t * 32, 32), 32)
        re, im = spec[at, :], spec[im_at, :]
        power = re * re + im * im
        top = power.astype(jnp.bfloat16)
        high[at, :] = top
        low[at, :] = (power - top.astype(jnp.float32)).astype(jnp.bfloat16)
        return carry

    lax.fori_loop(0, BINS // 32, powers, 0)

    place_ch = pl.ds(pl.multiple_of(chan * 64 + freq * 16, 16), 16)
    place_k = pl.ds(pl.multiple_of(win * 128, 128), 128)

    def white_of(d, h):
        return white.at[pl.ds(d[2] * 128 + (d[0] * 4 + d[1]) * 4 + 2 * h, 2)]

    def send_white(h, d):
        pltpu.make_async_remote_copy(
            src_ref=white_of(d, h),
            dst_ref=a_mat.at[pl.ds(2 * h, 2), place_ch, place_k],
            send_sem=send3, recv_sem=recv3.at[h], device_id=d, device_id_type=MESH,
        ).start()

    def send_share(i, h):
        each_peer(
            16, functools.partial(peer_share, i), functools.partial(send_white, h), i == 0)

    left = lax.broadcasted_iota(jnp.int32, (128, 128), 1) < 64

    def whiten(i, carry):
        t = (freq + i) % 4
        first = t * 128
        start = jnp.clip(first - 64, 0, BINS - 256)
        window = pl.ds(pl.multiple_of(start, 64), 256)
        apart = (lax.broadcasted_iota(jnp.int32, (128, 256), 1) + start) - (
            lax.broadcasted_iota(jnp.int32, (128, 256), 0) + first)
        band = jnp.where((apart >= -MARGIN) & (apart <= MARGIN), 1.0, 0.0).astype(jnp.bfloat16)
        smooth = (
            jnp.dot(band, high[window, :], preferred_element_type=jnp.float32)
            + jnp.dot(band, low[window, :], preferred_element_type=jnp.float32)
        ) / (2 * MARGIN + 1)
        scale = lax.rsqrt(smooth + 1e-06)
        re = spec[pl.ds(pl.multiple_of(first, 128), 128), :] * scale
        im = spec[pl.ds(pl.multiple_of(BINS + first, 128), 128), :] * scale
        for c in range(8):
            a, b = re[:, c * 128:(c + 1) * 128], im[:, c * 128:(c + 1) * 128]
            mixed[pl.ds(2 * c, 128, stride=16), :] = jnp.where(left, a, pltpu.roll(b, 64, 1))
            mixed[pl.ds(2 * c + 1, 128, stride=16), :] = jnp.where(left, pltpu.roll(a, 64, 1), b)
        white[pl.ds(pl.multiple_of(first, 128), 128)] = (
            mixed[...].reshape(128, 16, 128).astype(jnp.bfloat16))
        send_share(i, 0)
        return carry

    pl.semaphore_wait(in_sem.at[2], 3)
    lax.fori_loop(0, BINS // 128, whiten, 0)
    for h in range(2):
        pltpu.make_async_copy(
            white_of((chan, win, freq), h), a_mat.at[pl.ds(2 * h, 2), place_ch, place_k],
            recv3.at[h],
        ).start()

    def send_rest(i, carry):
        send_share(i, 1)
        return carry

    lax.fori_loop(0, 4, send_rest, 0)

    sign = jnp.where(lax.broadcasted_iota(jnp.int32, (64, 128), 1) < 64, 1.0, -1.0)

    def cross(b, carry):
        def multiply(m, c):
            for h in range(2):
                block = a_mat[b, pl.ds(pl.multiple_of(m * 128 + h * 64, 64), 64), :]
                b_mat[h * 128:h * 128 + 64, :] = block
                for w in range(4):
                    part = block[:, w * 128:(w + 1) * 128].astype(jnp.float32)
                    b_mat[h * 128 + 64:h * 128 + 128, w * 128:(w + 1) * 128] = (
                        pltpu.roll(part, 64, 1) * sign).astype(jnp.bfloat16)
            tile = lax.dot_general(
                a_mat[b], b_mat[...], NT, preferred_element_type=jnp.float32)
            tile = (tile * (1.0 / SEGMENTS)).astype(jnp.bfloat16)
            for h in range(2):
                sums[:, b, m * 2 + h] = tile[:, h * 128:(h + 1) * 128].reshape(32, 16, 128)
            return c

        lax.fori_loop(0, 4, multiply, 0)

        def send_sums(d):
            pltpu.make_async_remote_copy(
                src_ref=sums.at[d[0] * 4 + d[1], b],
                dst_ref=out_ref.at[holder * 4 + b],
                send_sem=send5, recv_sem=recv5, device_id=d, device_id_type=MESH,
            ).start()

        each_peer(16, peer_rows, send_sums)
        pltpu.make_async_copy(sums.at[holder, b], out_ref.at[holder * 4 + b], recv5).start()
        return carry

    for h in range(2):
        half = a_mat.at[pl.ds(2 * h, 2)]
        pltpu.make_async_copy(half, half, recv3.at[h]).wait()
        lax.fori_loop(2 * h, 2 * h + 2, cross, 0)

    pltpu.make_async_copy(out_ref, out_ref, recv5).wait()
    pltpu.make_async_copy(got.at[pl.ds(0, 48)], got.at[pl.ds(0, 48)], send1).wait()
    pltpu.make_async_copy(white.at[pl.ds(0, 508)], white.at[pl.ds(0, 508)], send3).wait()
    pltpu.make_async_copy(sums.at[pl.ds(0, 31)], sums.at[pl.ds(0, 31)], send5).wait()


def order_kernel(partner_ref, in_ref, out_ref, held, wide, in_sem, out_sem):
    chan = lax.axis_index("chan")
    parts = in_sem.shape[0]
    size = in_ref.shape[0] // parts

    def fetch(i):
        span = pl.ds(i * size, size)
        return pltpu.make_async_copy(in_ref.at[span], held.at[span], in_sem.at[i])

    for i in range(parts):
        fetch(i).start()

    def body(i, carry):
        span = pl.ds(i * size, size)
        fetch(i).wait()
        for r in range(8):
            wide[r, span] = held[span, partner_ref[r, chan]].astype(jnp.float32)
        pltpu.make_async_copy(wide.at[:, span], out_ref.at[0, :, span], out_sem).start()
        return carry

    lax.fori_loop(0, parts, body, 0)
    pltpu.make_async_copy(wide, out_ref.at[0], out_sem).wait()


def per_device(samples, partner):
    table = jnp.asarray(tables())
    sums = pl.pallas_call(
        main_kernel,
        out_shape=jax.ShapeDtypeStruct((128, 8, 16, 128), jnp.bfloat16),
        in_specs=[pl.BlockSpec(memory_space=pl.ANY)] * 2,
        out_specs=pl.BlockSpec(memory_space=pl.ANY),
        scratch_shapes=[
            pltpu.VMEM((2 * BINS, LENGTH), jnp.bfloat16),
            pltpu.VMEM((SEGS, 16, LENGTH), jnp.bfloat16),
            pltpu.VMEM((ROWS, 128), jnp.float32),
            pltpu.VMEM((ROWS, LENGTH), jnp.bfloat16),
            pltpu.VMEM((2 * BINS, ROWS), jnp.float32),
            pltpu.VMEM((BINS, ROWS), jnp.bfloat16),
            pltpu.VMEM((BINS, ROWS), jnp.bfloat16),
            pltpu.VMEM((128 * 16, 128), jnp.float32),
            pltpu.VMEM((BINS, 16, 128), jnp.bfloat16),
            pltpu.VMEM((4, CHANS, 512), jnp.bfloat16),
            pltpu.VMEM((256, 512), jnp.bfloat16),
            pltpu.VMEM((32, 4, 8, 16, 128), jnp.bfloat16),
        ] + [
            pltpu.SemaphoreType.DMA, pltpu.SemaphoreType.DMA, pltpu.SemaphoreType.DMA((4,))
        ] + [
            pltpu.SemaphoreType.DMA, pltpu.SemaphoreType.DMA((2,)),
            pltpu.SemaphoreType.DMA, pltpu.SemaphoreType.DMA, pltpu.SemaphoreType.REGULAR((3,))],
        compiler_params=pltpu.CompilerParams(
            collective_id=0, has_side_effects=True, vmem_limit_bytes=60 * 2**20),
        name="spectra",
    )(samples, table)
    return pl.pallas_call(
        order_kernel,
        out_shape=jax.ShapeDtypeStruct((1, 8, 128, 16, 128), jnp.float32),
        in_specs=[
            pl.BlockSpec(memory_space=pltpu.SMEM), pl.BlockSpec(memory_space=pl.ANY)],
        out_specs=pl.BlockSpec(memory_space=pl.ANY),
        scratch_shapes=[
            pltpu.VMEM((128, 8, 16, 128), jnp.bfloat16),
            pltpu.VMEM((8, 128, 16, 128), jnp.float32),
            pltpu.SemaphoreType.DMA((16,)),
            pltpu.SemaphoreType.DMA,
        ],
        compiler_params=pltpu.CompilerParams(vmem_limit_bytes=60 * 2**20),
        name="order",
    )(partner, sums)


def solution(mesh):
    in_specs = (P("win", "chan", "freq"), P())
    out_specs = P("chan", None, "freq", "win", None)
    return jax.shard_map(
        per_device, mesh=mesh, in_specs=in_specs, out_specs=out_specs, check_vma=False
    )
```

time: 140 us -> 113 us (0.81)
  Pallas kernels: 133 us -> 112 us
  local copies, waits for them, and re-layouts: 5.37 us -> 0 us
    pallas_call x1, Pallas kernels: 128 us -> 107 us  [per_device(): pl.pallas_call(main_kernel, out_shape=jax.ShapeDtypeStruct((128, 8, 16, 1...]
    unnamed x8 -> x0, local copies, waits for them, and re-layouts: 5.37 us -> none
where the time goes in v2:
time: 113 us; the launch traced here: 112 us
  Pallas kernels  112 us (99%)
    pallas_call x1, Pallas kernels, per_device(): pl.pallas_call(main_kernel, out_shape=jax.ShapeDtypeStruct((128, 8, 16, 1...  107 us
    pallas_call x1, Pallas kernels, per_device(): pl.pallas_call(order_kernel, out_shape=jax.ShapeDtypeStruct((1, 8, 128, 1...  5.13 us

profile of v2, /device:TPU:0, one launch (start us, length us, event | category | flops | bytes accessed | tf_op | source)
XLA Modules:
  0.0 111.9 jit_solution(3634329980737125829)
XLA Ops:
  0.0 106.7 %spectra.1.in_ref = bf16[128,8,16,128]{3,2,1,0:T(8,128)(2,1)} custom-call(bf16[64,64,256]{2,1,0:T(8,128)(2,1)} %x_ref.1, bf16[1024,1024]{1,0:T(8,128)(2,1)} %constant.2.clone.table_ref), custom_call_target="tpu_custom_call" | custom-call | tf_op jit(solution)/shard_map/spectra/pallas_call | solution.py:307
  106.8 5.1 %order.1 = f32[1,8,128,16,128]{4,3,2,1,0:T(8,128)} custom-call(s32[8,8]{1,0:T(8,128)} %partner_ref.1, bf16[128,8,16,128]{3,2,1,0:T(8,128)(2,1)} %spectra.1.in_ref), custom_call_target="tpu_custom_call" | custom-call | tf_op jit(solution)/shard_map/order/pallas_call | solution.py:334

commit v3 on v2

--- a/solution.py
+++ b/solution.py
@@ -1,4 +1,3 @@
-import functools
 import math
 
 import jax
@@ -36,50 +35,15 @@
     return chan // 4, chan % 4, win, freq // 2, freq % 2
 
 
-def peer_all(i, s):
-    y_hi, x, z, y_lo, core = position()
-    y = (y_hi * 2 + y_lo + i // 2 % 2 + 2 * s) % 4
-    return (
-        (y // 2) * 4 + (x + i // 4 % 4 + 2 * s) % 4,
-        (z + i // 16 + 2 * s) % 4,
-        y % 2 * 2 + (core + i % 2) % 2,
-    )
-
-
-def peer_rows(i, s):
-    y_hi, x, z, y_lo, core = position()
-    return (
-        (y_hi + s) % 2 * 4 + (x + i % 4 + 2 * s) % 4,
-        (z + i // 4 + 2 * s) % 4,
-        y_lo * 2 + core,
-    )
-
-
-def peer_share(k, i, s):
-    y_hi, x, z, y_lo, core = position()
-    y = (y_hi * 2 + (y_lo * 2 + core + k) % 4 // 2 + 2 * s) % 4
-    return (
-        y // 2 * 4 + (x + i % 4 + 2 * s) % 4,
-        (z + i // 4 + 2 * s) % 4,
-        (y_lo * 2 + core + k) % 4,
-    )
-
-
-def each_peer(half, peer, act, skip_own=True):
-    if skip_own is not True:
-
-        @pl.when(jnp.logical_not(skip_own))
-        def _():
-            act(peer(0, 0))
-
-    act(peer(0, 1))
-
-    def body(i, carry):
-        act(peer(i, 0))
-        act(peer(i, 1))
-        return carry
-
-    lax.fori_loop(1, half, body, 0)
+def spread(freq):
+    y_hi, x, z, _, _ = position()
+    halves = y_hi, 1 - y_hi
+    xs = [(x + i) % 4 for i in range(4)]
+    zs = [(z + i) % 4 for i in range(4)]
+    return [
+        (halves[s] * 4 + xs[(i + 2 * s) % 4], zs[(j + 2 * s) % 4], freq)
+        for j in range(4) for i in range(4) for s in range(2)
+    ]
 
 
 def main_kernel(
@@ -162,22 +126,34 @@
     transform(y_lo * 2, 2, True)
     pl.semaphore_wait(in_sem.at[1], 3)
     tell(in_sem.at[2], along_freq)
-    for i in (2, 3):
-        arrived(i)
-        reorder(across(i))
-        transform(across(i), 1, False)
-
-    def powers(t, carry):
-        at = pl.ds(pl.multiple_of(t * 32, 32), 32)
-        im_at = pl.ds(pl.multiple_of(BINS + t * 32, 32), 32)
-        re, im = spec[at, :], spec[im_at, :]
-        power = re * re + im * im
-        top = power.astype(jnp.bfloat16)
-        high[at, :] = top
-        low[at, :] = (power - top.astype(jnp.float32)).astype(jnp.bfloat16)
-        return carry
-
-    lax.fori_loop(0, BINS // 32, powers, 0)
+    arrived(2)
+    reorder(across(2))
+    transform(across(2), 1, False)
+    arrived(3)
+    reorder(across(3))
+
+    def finish(half):
+        span = stretch(across(3))
+        re_at = pl.ds(pl.multiple_of(half * 256, 256), 256)
+        im_at = pl.ds(pl.multiple_of(BINS + half * 256, 256), 256)
+
+        def body(t, carry):
+            at = pl.ds(pl.multiple_of(t * 256, 256), 256)
+
+            def total(part):
+                return spec[part, at] + lax.dot_general(
+                    table[part, span], rows[at, span], NT, preferred_element_type=jnp.float32)
+
+            re, im = total(re_at), total(im_at)
+            spec[re_at, at] = re
+            spec[im_at, at] = im
+            power = re * re + im * im
+            top = power.astype(jnp.bfloat16)
+            high[re_at, at] = top
+            low[re_at, at] = (power - top.astype(jnp.float32)).astype(jnp.bfloat16)
+            return carry
+
+        lax.fori_loop(0, ROWS // 256, body, 0)
 
     place_ch = pl.ds(pl.multiple_of(chan * 64 + freq * 16, 16), 16)
     place_k = pl.ds(pl.multiple_of(win * 128, 128), 128)
@@ -192,14 +168,19 @@
             send_sem=send3, recv_sem=recv3.at[h], device_id=d, device_id_type=MESH,
         ).start()
 
-    def send_share(i, h):
-        each_peer(
-            16, functools.partial(peer_share, i), functools.partial(send_white, h), i == 0)
+    def turn(i):
+        return y_lo * 3 + (1 - 2 * y_lo) * i
+
+    def send_share(t, h):
+        own, *others = spread(t)
+        pl.when(t != freq)(lambda: send_white(h, own))
+        for d in others:
+            send_white(h, d)
 
     left = lax.broadcasted_iota(jnp.int32, (128, 128), 1) < 64
 
     def whiten(i, carry):
-        t = (freq + i) % 4
+        t = turn(i)
         first = t * 128
         start = jnp.clip(first - 64, 0, BINS - 256)
         window = pl.ds(pl.multiple_of(start, 64), 256)
@@ -219,11 +200,14 @@
             mixed[pl.ds(2 * c + 1, 128, stride=16), :] = jnp.where(left, pltpu.roll(a, 64, 1), b)
         white[pl.ds(pl.multiple_of(first, 128), 128)] = (
             mixed[...].reshape(128, 16, 128).astype(jnp.bfloat16))
-        send_share(i, 0)
+        send_share(t, 0)
         return carry
 
+    finish(y_lo)
     pl.semaphore_wait(in_sem.at[2], 3)
-    lax.fori_loop(0, BINS // 128, whiten, 0)
+    whiten(0, 0)
+    finish(1 - y_lo)
+    lax.fori_loop(1, BINS // 128, whiten, 0)
     for h in range(2):
         pltpu.make_async_copy(
             white_of((chan, win, freq), h), a_mat.at[pl.ds(2 * h, 2), place_ch, place_k],
@@ -231,7 +215,7 @@
         ).start()
 
     def send_rest(i, carry):
-        send_share(i, 1)
+        send_share(turn(i), 1)
         return carry
 
     lax.fori_loop(0, 4, send_rest, 0)
@@ -263,7 +247,8 @@
                 send_sem=send5, recv_sem=recv5, device_id=d, device_id_type=MESH,
             ).start()
 
-        each_peer(16, peer_rows, send_sums)
+        for d in spread(freq)[1:]:
+            send_sums(d)
         pltpu.make_async_copy(sums.at[holder, b], out_ref.at[holder * 4 + b], recv5).start()
         return carry
 
@@ -278,23 +263,15 @@
     pltpu.make_async_copy(sums.at[pl.ds(0, 31)], sums.at[pl.ds(0, 31)], send5).wait()
 
 
-def order_kernel(partner_ref, in_ref, out_ref, held, wide, in_sem, out_sem):
+def order_kernel(partner_ref, in_ref, out_ref, wide, out_sem):
     chan = lax.axis_index("chan")
-    parts = in_sem.shape[0]
+    parts = 8
     size = in_ref.shape[0] // parts
-
-    def fetch(i):
-        span = pl.ds(i * size, size)
-        return pltpu.make_async_copy(in_ref.at[span], held.at[span], in_sem.at[i])
-
-    for i in range(parts):
-        fetch(i).start()
 
     def body(i, carry):
         span = pl.ds(i * size, size)
-        fetch(i).wait()
         for r in range(8):
-            wide[r, span] = held[span, partner_ref[r, chan]].astype(jnp.float32)
+            wide[r, span] = in_ref[span, partner_ref[r, chan]].astype(jnp.float32)
         pltpu.make_async_copy(wide.at[:, span], out_ref.at[0, :, span], out_sem).start()
         return carry
 
@@ -306,9 +283,9 @@
     table = jnp.asarray(tables())
     sums = pl.pallas_call(
         main_kernel,
-        out_shape=jax.ShapeDtypeStruct((128, 8, 16, 128), jnp.bfloat16),
+        out_shape=pltpu.VMEM((128, 8, 16, 128), jnp.bfloat16),
         in_specs=[pl.BlockSpec(memory_space=pl.ANY)] * 2,
-        out_specs=pl.BlockSpec(memory_space=pl.ANY),
+        out_specs=pl.BlockSpec(memory_space=pltpu.VMEM),
         scratch_shapes=[
             pltpu.VMEM((2 * BINS, LENGTH), jnp.bfloat16),
             pltpu.VMEM((SEGS, 16, LENGTH), jnp.bfloat16),
@@ -328,22 +305,20 @@
             pltpu.SemaphoreType.DMA, pltpu.SemaphoreType.DMA((2,)),
             pltpu.SemaphoreType.DMA, pltpu.SemaphoreType.DMA, pltpu.SemaphoreType.REGULAR((3,))],
         compiler_params=pltpu.CompilerParams(
-            collective_id=0, has_side_effects=True, vmem_limit_bytes=60 * 2**20),
+            collective_id=0, has_side_effects=True, vmem_limit_bytes=50 * 2**20),
         name="spectra",
     )(samples, table)
     return pl.pallas_call(
         order_kernel,
         out_shape=jax.ShapeDtypeStruct((1, 8, 128, 16, 128), jnp.float32),
         in_specs=[
-            pl.BlockSpec(memory_space=pltpu.SMEM), pl.BlockSpec(memory_space=pl.ANY)],
+            pl.BlockSpec(memory_space=pltpu.SMEM), pl.BlockSpec(memory_space=pltpu.VMEM)],
         out_specs=pl.BlockSpec(memory_space=pl.ANY),
         scratch_shapes=[
-            pltpu.VMEM((128, 8, 16, 128), jnp.bfloat16),
             pltpu.VMEM((8, 128, 16, 128), jnp.float32),
-            pltpu.SemaphoreType.DMA((16,)),
             pltpu.SemaphoreType.DMA,
         ],
-        compiler_params=pltpu.CompilerParams(vmem_limit_bytes=60 * 2**20),
+        compiler_params=pltpu.CompilerParams(vmem_limit_bytes=20 * 2**20),
         name="order",
     )(partner, sums)
 

time: 113 us -> 110 us (0.973)
  Pallas kernels: 112 us -> 109 us
    pallas_call x1, Pallas kernels: 107 us -> 105 us  [per_device(): pl.pallas_call(main_kernel, out_shape=pltpu.VMEM((128, 8, 16, 128), jnp.b...]
    pallas_call x1, Pallas kernels: 5.13 us -> 3.99 us  [per_device(): pl.pallas_call(order_kernel, out_shape=jax.ShapeDtypeStruct((1, 8, 128, 1...]
where the time goes in v3:
time: 110 us; the launch traced here: 109 us
  Pallas kernels  109 us (99%)
    pallas_call x1, Pallas kernels, per_device(): pl.pallas_call(main_kernel, out_shape=pltpu.VMEM((128, 8, 16, 128), jnp.b...  105 us
    pallas_call x1, Pallas kernels, per_device(): pl.pallas_call(order_kernel, out_shape=jax.ShapeDtypeStruct((1, 8, 128, 1...  3.99 us

profile of v3, /device:TPU:0, one launch (start us, length us, event | category | flops | bytes accessed | tf_op | source)
XLA Modules:
  0.0 109.0 jit_solution(2257123762925615650)
XLA Ops:
  0.0 0.0 copy-start
  0.0 105.0 %spectra.1.in_ref = bf16[128,8,16,128]{3,2,1,0:T(8,128)(2,1)S(1)} custom-call(bf16[64,64,256]{2,1,0:T(8,128)(2,1)} %x_ref.1, bf16[1024,1024]{1,0:T(8,128)(2,1)} %constant.2.clone.table_ref), custom_call_target="tpu_custom_call" | custom-call | tf_op jit(solution)/shard_map/spectra/pallas_call | solution.py:284
  105.0 0.0 copy-done
  105.0 4.0 %order.1 = f32[1,8,128,16,128]{4,3,2,1,0:T(8,128)} custom-call(s32[8,8]{1,0:T(8,128)S(1)} %copy-done, bf16[128,8,16,128]{3,2,1,0:T(8,128)(2,1)S(1)} %spectra.1.in_ref), custom_call_target="tpu_custom_call" | custom-call | tf_op jit(solution)/shard_map/order/pallas_call | solution.py:311
Async XLA Ops:
  0.0 105.0 %copy-start = (s32[8,8]{1,0:T(8,128)S(1)}, s32[8,8]{1,0:T(8,128)}, u32[]{:S(2)}) copy-start(s32[8,8]{1,0:T(8,128)} %partner_ref.1) | copy-start | bytes 772

commit v4 on v3

--- a/solution.py
+++ b/solution.py
@@ -76,11 +76,7 @@
     def stretch(k, size=1):
         return pl.ds(pl.multiple_of(k * piece, size * piece), size * piece)
 
-    pltpu.make_async_copy(
-        x_ref.at[:, pl.ds(pl.multiple_of(freq * 16, 16), 16), :],
-        got.at[:, :, stretch(freq)], recv1.at[0],
-    ).start()
-    for i in (2, 1, 3):
+    for i in (2, 3, 1):
         k = across(i)
         pltpu.make_async_remote_copy(
             src_ref=x_ref.at[:, pl.ds(pl.multiple_of(k * 16, 16), 16), :],
@@ -88,6 +84,11 @@
             send_sem=send1, recv_sem=recv1.at[i],
             device_id=(chan, win, k), device_id_type=MESH,
         ).start()
+
+    pltpu.make_async_copy(
+        x_ref.at[:, pl.ds(pl.multiple_of(freq * 16, 16), 16), :],
+        got.at[:, :, stretch(freq)], recv1.at[0],
+    ).start()
 
     def arrived(i):
         part = got.at[:, :, stretch(across(i))]
@@ -201,6 +202,7 @@
         white[pl.ds(pl.multiple_of(first, 128), 128)] = (
             mixed[...].reshape(128, 16, 128).astype(jnp.bfloat16))
         send_share(t, 0)
+        send_share(t, 1)
         return carry
 
     finish(y_lo)
@@ -213,12 +215,6 @@
             white_of((chan, win, freq), h), a_mat.at[pl.ds(2 * h, 2), place_ch, place_k],
             recv3.at[h],
         ).start()
-
-    def send_rest(i, carry):
-        send_share(turn(i), 1)
-        return carry
-
-    lax.fori_loop(0, 4, send_rest, 0)
 
     sign = jnp.where(lax.broadcasted_iota(jnp.int32, (64, 128), 1) < 64, 1.0, -1.0)
 

time: 110 us -> 109 us (level); the launches traced: 109 us -> 109 us
  no operation moved by 1% of the time
where the time goes in v4:
time: 109 us
  Pallas kernels  109 us (100%)
    pallas_call x1, Pallas kernels, per_device(): pl.pallas_call(main_kernel, out_shape=pltpu.VMEM((128, 8, 16, 128), jnp.b...  105 us
    pallas_call x1, Pallas kernels, per_device(): pl.pallas_call(order_kernel, out_shape=jax.ShapeDtypeStruct((1, 8, 128, 1...  3.99 us

profile of v4, /device:TPU:0, one launch (start us, length us, event | category | flops | bytes accessed | tf_op | source)
XLA Modules:
  0.0 109.1 jit_solution(7608827387357438186)
XLA Ops:
  0.0 0.0 copy-start
  0.0 105.1 %spectra.1.in_ref = bf16[128,8,16,128]{3,2,1,0:T(8,128)(2,1)S(1)} custom-call(bf16[64,64,256]{2,1,0:T(8,128)(2,1)} %x_ref.1, bf16[1024,1024]{1,0:T(8,128)(2,1)} %constant.2.clone.table_ref), custom_call_target="tpu_custom_call" | custom-call | tf_op jit(solution)/shard_map/spectra/pallas_call | solution.py:280
  105.1 0.0 copy-done
  105.1 4.0 %order.1 = f32[1,8,128,16,128]{4,3,2,1,0:T(8,128)} custom-call(s32[8,8]{1,0:T(8,128)S(1)} %copy-done, bf16[128,8,16,128]{3,2,1,0:T(8,128)(2,1)S(1)} %spectra.1.in_ref), custom_call_target="tpu_custom_call" | custom-call | tf_op jit(solution)/shard_map/order/pallas_call | solution.py:307
Async XLA Ops:
  0.0 105.1 %copy-start = (s32[8,8]{1,0:T(8,128)S(1)}, s32[8,8]{1,0:T(8,128)}, u32[]{:S(2)}) copy-start(s32[8,8]{1,0:T(8,128)} %partner_ref.1) | copy-start | bytes 772

commit v5 on v4

--- a/solution.py
+++ b/solution.py
@@ -97,7 +97,7 @@
     def reorder(k):
         def body(c, carry):
             at = pl.ds(pl.multiple_of(k * piece + c * 128, 128), 128)
-            wide[...] = got[:, :, at].astype(jnp.float32).reshape(ROWS, 128)
+            wide[:ROWS, :] = got[:, :, at].astype(jnp.float32).reshape(ROWS, 128)
             for ch in range(16):
                 rows[ch * 64:(ch + 1) * 64, at] = (
                     wide[pl.ds(ch, 64, stride=16), :].astype(jnp.bfloat16))
@@ -200,7 +200,7 @@
             mixed[pl.ds(2 * c, 128, stride=16), :] = jnp.where(left, a, pltpu.roll(b, 64, 1))
             mixed[pl.ds(2 * c + 1, 128, stride=16), :] = jnp.where(left, pltpu.roll(a, 64, 1), b)
         white[pl.ds(pl.multiple_of(first, 128), 128)] = (
-            mixed[...].reshape(128, 16, 128).astype(jnp.bfloat16))
+            mixed[:128 * 16, :].reshape(128, 16, 128).astype(jnp.bfloat16))
         send_share(t, 0)
         send_share(t, 1)
         return carry
@@ -268,7 +268,7 @@
         span = pl.ds(i * size, size)
         for r in range(8):
             wide[r, span] = in_ref[span, partner_ref[r, chan]].astype(jnp.float32)
-        pltpu.make_async_copy(wide.at[:, span], out_ref.at[0, :, span], out_sem).start()
+            pltpu.make_async_copy(wide.at[r, span], out_ref.at[0, r, span], out_sem).start()
         return carry
 
     lax.fori_loop(0, parts, body, 0)
@@ -285,12 +285,12 @@
         scratch_shapes=[
             pltpu.VMEM((2 * BINS, LENGTH), jnp.bfloat16),
             pltpu.VMEM((SEGS, 16, LENGTH), jnp.bfloat16),
-            pltpu.VMEM((ROWS, 128), jnp.float32),
+            pltpu.VMEM((ROWS + 16, 128), jnp.float32),
             pltpu.VMEM((ROWS, LENGTH), jnp.bfloat16),
             pltpu.VMEM((2 * BINS, ROWS), jnp.float32),
             pltpu.VMEM((BINS, ROWS), jnp.bfloat16),
             pltpu.VMEM((BINS, ROWS), jnp.bfloat16),
-            pltpu.VMEM((128 * 16, 128), jnp.float32),
+            pltpu.VMEM((128 * 16 + 16, 128), jnp.float32),
             pltpu.VMEM((BINS, 16, 128), jnp.bfloat16),
             pltpu.VMEM((4, CHANS, 512), jnp.bfloat16),
             pltpu.VMEM((256, 512), jnp.bfloat16),

time: 109 us -> 109 us (level)
  no operation moved by 1% of the time
where the time goes in v5:
time: 109 us
  Pallas kernels  109 us (100%)
    pallas_call x1, Pallas kernels, per_device(): pl.pallas_call(main_kernel, out_shape=pltpu.VMEM((128, 8, 16, 128), jnp.b...  105 us
    pallas_call x1, Pallas kernels, per_device(): pl.pallas_call(order_kernel, out_shape=jax.ShapeDtypeStruct((1, 8, 128, 1...  3.86 us

profile of v5, /device:TPU:0, one launch (start us, length us, event | category | flops | bytes accessed | tf_op | source)
XLA Modules:
  0.0 109.0 jit_solution(5471711039927367224)
XLA Ops:
  0.0 0.0 copy-start
  0.0 105.1 %spectra.1.in_ref = bf16[128,8,16,128]{3,2,1,0:T(8,128)(2,1)S(1)} custom-call(bf16[64,64,256]{2,1,0:T(8,128)(2,1)} %x_ref.1, bf16[1024,1024]{1,0:T(8,128)(2,1)} %constant.2.clone.table_ref), custom_call_target="tpu_custom_call" | custom-call | tf_op jit(solution)/shard_map/spectra/pallas_call | solution.py:280
  105.1 0.0 copy-done
  105.1 3.9 %order.1 = f32[1,8,128,16,128]{4,3,2,1,0:T(8,128)} custom-call(s32[8,8]{1,0:T(8,128)S(1)} %copy-done, bf16[128,8,16,128]{3,2,1,0:T(8,128)(2,1)S(1)} %spectra.1.in_ref), custom_call_target="tpu_custom_call" | custom-call | tf_op jit(solution)/shard_map/order/pallas_call | solution.py:307
Async XLA Ops:
  0.0 105.1 %copy-start = (s32[8,8]{1,0:T(8,128)S(1)}, s32[8,8]{1,0:T(8,128)}, u32[]{:S(2)}) copy-start(s32[8,8]{1,0:T(8,128)} %partner_ref.1) | copy-start | bytes 772

commit v6 on v5

--- a/solution.py
+++ b/solution.py
@@ -76,12 +76,16 @@
     def stretch(k, size=1):
         return pl.ds(pl.multiple_of(k * piece, size * piece), size * piece)
 
-    for i in (2, 3, 1):
+    def part(k, j, parts):
+        size = piece // parts
+        return pl.ds(pl.multiple_of(k * piece + j * size, size), size)
+
+    for i, j, parts in ((2, 0, 1), (3, 0, 2), (3, 1, 2), (1, 0, 1)):
         k = across(i)
         pltpu.make_async_remote_copy(
-            src_ref=x_ref.at[:, pl.ds(pl.multiple_of(k * 16, 16), 16), :],
-            dst_ref=got.at[:, :, stretch(freq)],
-            send_sem=send1, recv_sem=recv1.at[i],
+            src_ref=x_ref.at[:, pl.ds(pl.multiple_of(k * 16, 16), 16), part(0, j, parts)],
+            dst_ref=got.at[:, :, part(freq, j, parts)],
+            send_sem=send1, recv_sem=recv1.at[i + j],
             device_id=(chan, win, k), device_id_type=MESH,
         ).start()
 
@@ -90,11 +94,11 @@
         got.at[:, :, stretch(freq)], recv1.at[0],
     ).start()
 
-    def arrived(i):
-        part = got.at[:, :, stretch(across(i))]
-        pltpu.make_async_copy(part, part, recv1.at[i]).wait()
-
-    def reorder(k):
+    def arrived(i, j=0, parts=1):
+        here = got.at[:, :, part(across(i), j, parts)]
+        pltpu.make_async_copy(here, here, recv1.at[i + j]).wait()
+
+    def reorder(k, j=0, parts=1):
         def body(c, carry):
             at = pl.ds(pl.multiple_of(k * piece + c * 128, 128), 128)
             wide[:ROWS, :] = got[:, :, at].astype(jnp.float32).reshape(ROWS, 128)
@@ -103,7 +107,8 @@
                     wide[pl.ds(ch, 64, stride=16), :].astype(jnp.bfloat16))
             return carry
 
-        lax.fori_loop(0, piece // 128, body, 0)
+        each = piece // 128 // parts
+        lax.fori_loop(j * each, (j + 1) * each, body, 0)
 
     def transform(k, size, first):
         span = stretch(k, size)
@@ -130,8 +135,9 @@
     arrived(2)
     reorder(across(2))
     transform(across(2), 1, False)
-    arrived(3)
-    reorder(across(3))
+    for j in range(2):
+        arrived(3, j, 2)
+        reorder(across(3), j, 2)
 
     def finish(half):
         span = stretch(across(3))
@@ -296,7 +302,7 @@
             pltpu.VMEM((256, 512), jnp.bfloat16),
             pltpu.VMEM((32, 4, 8, 16, 128), jnp.bfloat16),
         ] + [
-            pltpu.SemaphoreType.DMA, pltpu.SemaphoreType.DMA, pltpu.SemaphoreType.DMA((4,))
+            pltpu.SemaphoreType.DMA, pltpu.SemaphoreType.DMA, pltpu.SemaphoreType.DMA((5,))
         ] + [
             pltpu.SemaphoreType.DMA, pltpu.SemaphoreType.DMA((2,)),
             pltpu.SemaphoreType.DMA, pltpu.SemaphoreType.DMA, pltpu.SemaphoreType.REGULAR((3,))],

time: 109 us -> 109 us (level)
  no operation moved by 1% of the time
where the time goes in v6:
time: 109 us
  Pallas kernels  109 us (100%)
    pallas_call x1, Pallas kernels, per_device(): pl.pallas_call(main_kernel, out_shape=pltpu.VMEM((128, 8, 16, 128), jnp.b...  105 us
    pallas_call x1, Pallas kernels, per_device(): pl.pallas_call(order_kernel, out_shape=jax.ShapeDtypeStruct((1, 8, 128, 1...  3.86 us

profile of v6, /device:TPU:0, one launch (start us, length us, event | category | flops | bytes accessed | tf_op | source)
XLA Modules:
  0.0 108.8 jit_solution(3134366596602572084)
XLA Ops:
  0.0 0.0 copy-start
  0.0 104.9 %spectra.1.in_ref = bf16[128,8,16,128]{3,2,1,0:T(8,128)(2,1)S(1)} custom-call(bf16[64,64,256]{2,1,0:T(8,128)(2,1)} %x_ref.1, bf16[1024,1024]{1,0:T(8,128)(2,1)} %constant.2.clone.table_ref), custom_call_target="tpu_custom_call" | custom-call | tf_op jit(solution)/shard_map/spectra/pallas_call | solution.py:286
  104.9 0.0 copy-done
  104.9 3.9 %order.1 = f32[1,8,128,16,128]{4,3,2,1,0:T(8,128)} custom-call(s32[8,8]{1,0:T(8,128)S(1)} %copy-done, bf16[128,8,16,128]{3,2,1,0:T(8,128)(2,1)S(1)} %spectra.1.in_ref), custom_call_target="tpu_custom_call" | custom-call | tf_op jit(solution)/shard_map/order/pallas_call | solution.py:313
Async XLA Ops:
  0.0 104.9 %copy-start = (s32[8,8]{1,0:T(8,128)S(1)}, s32[8,8]{1,0:T(8,128)}, u32[]{:S(2)}) copy-start(s32[8,8]{1,0:T(8,128)} %partner_ref.1) | copy-start | bytes 772

commit v7 on v6

--- a/solution.py
+++ b/solution.py
@@ -123,6 +123,8 @@
         lax.fori_loop(0, ROWS // 256, body, 0)
 
     tell(in_sem.at[0], along_z)
+    for powers in (high, low):
+        powers[192:320, :] = jnp.zeros((128, ROWS), jnp.bfloat16)
     take_table.wait()
     for i in (0, 1):
         arrived(i)
@@ -139,10 +141,10 @@
         arrived(3, j, 2)
         reorder(across(3), j, 2)
 
-    def finish(half):
+    def finish(first, size):
         span = stretch(across(3))
-        re_at = pl.ds(pl.multiple_of(half * 256, 256), 256)
-        im_at = pl.ds(pl.multiple_of(BINS + half * 256, 256), 256)
+        re_at = pl.ds(pl.multiple_of(first, 64), size)
+        im_at = pl.ds(pl.multiple_of(BINS + first, 64), size)
 
         def body(t, carry):
             at = pl.ds(pl.multiple_of(t * 256, 256), 256)
@@ -197,7 +199,7 @@
         smooth = (
             jnp.dot(band, high[window, :], preferred_element_type=jnp.float32)
             + jnp.dot(band, low[window, :], preferred_element_type=jnp.float32)
-        ) / (2 * MARGIN + 1)
+        ) * (1.0 / (2 * MARGIN + 1))
         scale = lax.rsqrt(smooth + 1e-06)
         re = spec[pl.ds(pl.multiple_of(first, 128), 128), :] * scale
         im = spec[pl.ds(pl.multiple_of(BINS + first, 128), 128), :] * scale
@@ -211,10 +213,10 @@
         send_share(t, 1)
         return carry
 
-    finish(y_lo)
+    finish(y_lo * 320, 192)
     pl.semaphore_wait(in_sem.at[2], 3)
     whiten(0, 0)
-    finish(1 - y_lo)
+    finish((1 - y_lo) * 192, 320)
     lax.fori_loop(1, BINS // 128, whiten, 0)
     for h in range(2):
         pltpu.make_async_copy(

time: 109 us -> 109 us (level)
  no operation moved by 1% of the time
where the time goes in v7:
time: 109 us
  Pallas kernels  109 us (100%)
    pallas_call x1, Pallas kernels, per_device(): pl.pallas_call(main_kernel, out_shape=pltpu.VMEM((128, 8, 16, 128), jnp.b...  105 us
    pallas_call x1, Pallas kernels, per_device(): pl.pallas_call(order_kernel, out_shape=jax.ShapeDtypeStruct((1, 8, 128, 1...  3.86 us

profile of v7, /device:TPU:0, one launch (start us, length us, event | category | flops | bytes accessed | tf_op | source)
XLA Modules:
  0.0 108.7 jit_solution(14674493509973923882)
XLA Ops:
  0.0 0.0 copy-start
  0.0 104.8 %spectra.1.in_ref = bf16[128,8,16,128]{3,2,1,0:T(8,128)(2,1)S(1)} custom-call(bf16[64,64,256]{2,1,0:T(8,128)(2,1)} %x_ref.1, bf16[1024,1024]{1,0:T(8,128)(2,1)} %constant.2.clone.table_ref), custom_call_target="tpu_custom_call" | custom-call | tf_op jit(solution)/shard_map/spectra/pallas_call | solution.py:288
  104.8 0.0 copy-done
  104.8 3.9 %order.1 = f32[1,8,128,16,128]{4,3,2,1,0:T(8,128)} custom-call(s32[8,8]{1,0:T(8,128)S(1)} %copy-done, bf16[128,8,16,128]{3,2,1,0:T(8,128)(2,1)S(1)} %spectra.1.in_ref), custom_call_target="tpu_custom_call" | custom-call | tf_op jit(solution)/shard_map/order/pallas_call | solution.py:315
Async XLA Ops:
  0.0 104.8 %copy-start = (s32[8,8]{1,0:T(8,128)S(1)}, s32[8,8]{1,0:T(8,128)}, u32[]{:S(2)}) copy-start(s32[8,8]{1,0:T(8,128)} %partner_ref.1) | copy-start | bytes 772

commit v8 on v6

--- a/solution.py
+++ b/solution.py
@@ -35,14 +35,18 @@
     return chan // 4, chan % 4, win, freq // 2, freq % 2
 
 
-def spread(freq):
+IN_TURN = [(i, j) for j in range(4) for i in range(4)]
+MIXED = [(0, 0)] + [(2, 2), (0, 1), (3, 1), (1, 3), (3, 2), (0, 2), (1, 2), (1, 1), (3, 0), (2, 1), (0, 3), (2, 0), (1, 0), (3, 3), (2, 3)]
+
+
+def spread(freq, order=IN_TURN):
     y_hi, x, z, _, _ = position()
     halves = y_hi, 1 - y_hi
     xs = [(x + i) % 4 for i in range(4)]
     zs = [(z + i) % 4 for i in range(4)]
     return [
         (halves[s] * 4 + xs[(i + 2 * s) % 4], zs[(j + 2 * s) % 4], freq)
-        for j in range(4) for i in range(4) for s in range(2)
+        for i, j in order for s in range(2)
     ]
 
 
@@ -249,7 +253,7 @@
                 send_sem=send5, recv_sem=recv5, device_id=d, device_id_type=MESH,
             ).start()
 
-        for d in spread(freq)[1:]:
+        for d in spread(freq, MIXED)[1:]:
             send_sums(d)
         pltpu.make_async_copy(sums.at[holder, b], out_ref.at[holder * 4 + b], recv5).start()
         return carry

time: 109 us -> 109 us (level)
  no operation moved by 1% of the time
where the time goes in v8:
time: 109 us; the launch traced here: 108 us
  Pallas kernels  108 us (99%)
    pallas_call x1, Pallas kernels, per_device(): pl.pallas_call(main_kernel, out_shape=pltpu.VMEM((128, 8, 16, 128), jnp.b...  105 us
    pallas_call x1, Pallas kernels, per_device(): pl.pallas_call(order_kernel, out_shape=jax.ShapeDtypeStruct((1, 8, 128, 1...  3.86 us

profile of v8, /device:TPU:0, one launch (start us, length us, event | category | flops | bytes accessed | tf_op | source)
XLA Modules:
  0.0 108.4 jit_solution(6511697267373300683)
XLA Ops:
  0.0 0.0 copy-start
  0.0 104.5 %spectra.1.in_ref = bf16[128,8,16,128]{3,2,1,0:T(8,128)(2,1)S(1)} custom-call(bf16[64,64,256]{2,1,0:T(8,128)(2,1)} %x_ref.1, bf16[1024,1024]{1,0:T(8,128)(2,1)} %constant.2.clone.table_ref), custom_call_target="tpu_custom_call" | custom-call | tf_op jit(solution)/shard_map/spectra/pallas_call | solution.py:290
  104.6 0.0 copy-done
  104.6 3.9 %order.1 = f32[1,8,128,16,128]{4,3,2,1,0:T(8,128)} custom-call(s32[8,8]{1,0:T(8,128)S(1)} %copy-done, bf16[128,8,16,128]{3,2,1,0:T(8,128)(2,1)S(1)} %spectra.1.in_ref), custom_call_target="tpu_custom_call" | custom-call | tf_op jit(solution)/shard_map/order/pallas_call | solution.py:317
Async XLA Ops:
  0.0 104.6 %copy-start = (s32[8,8]{1,0:T(8,128)S(1)}, s32[8,8]{1,0:T(8,128)}, u32[]{:S(2)}) copy-start(s32[8,8]{1,0:T(8,128)} %partner_ref.1) | copy-start | bytes 772
